TPU v7x, 128 devices: a whole 4x4x4 slice. The times are simulated.
128 devices in a mesh: seq: 8 (over x, y_lo), fsdp: 16 (over z, y_hi, core).
Axes of the slice: x: 4, y: 4 (y_hi: 2, y_lo: 2; y = y_hi * 2 + y_lo), z: 4, core: 2. Of those that a mesh axis runs over, the one named last changes fastest.
Arguments:
- tokens: bfloat16 [16, 1024, 1152], P('fsdp', 'seq'), may hold values from -6 to 6
- w_attn: bfloat16 [1152, 2560], P('fsdp'), may hold values from -0.1875 to 0.1875
- w_mlp: bfloat16 [1152, 20736], P('fsdp'), may hold values from -0.1875 to 0.1875
- norm_gains: bfloat16 [4, 1152], P(None, 'fsdp'), may hold values from 0.25 to 1.75
- qk_gains: bfloat16 [2, 256], P(None, 'fsdp'), may hold values from 0.25 to 1.75
- cotangent: bfloat16 [16, 1024, 1152], P('fsdp', 'seq'), may hold values from -6 to 6
Outputs:
- result: bfloat16 [16, 1024, 1152], P('fsdp', 'seq')
- tokens_grad: float32 [16, 1024, 1152], P('fsdp', 'seq')
- w_attn_grad: float32 [1152, 2560], P('fsdp')
- w_mlp_grad: float32 [1152, 20736], P('fsdp')
- norm_gains_grad: float32 [4, 1152], P(None, 'fsdp')
- qk_gains_grad: float32 [2, 256], P(None, 'fsdp')
All inputs are finite; a program needn't handle non-finite values.
Results may differ from a plain program's by a relative error of at most 0.025.
Values may be sent and summed in bfloat16 or wider, within the bound.
A program may use at most 320 MiB of HBM per device.

v0:
```python
from functools import partial

import jax
import jax.numpy as jnp
from jax import lax
from jax.sharding import PartitionSpec as P

HEADS = 4
HEAD = 256
FF = 6912
WINDOW = 512


EPSILON = 1e-06
ROPE_BASE = 10000.0
MASKED = -1e30


def passed_along(value, axis, steps):
    count = lax.axis_size(axis)
    initial, last = (max(0, -steps), min(count, count - steps))
    return lax.ppermute(value, axis, [(source, source + steps) for source in range(initial, last)])


def inverse_rms(values):
    return lax.rsqrt(jnp.mean(values * values, axis=-1, keepdims=True) + EPSILON)


def rms_back(grad_normed, normed, inverse):
    return inverse * (grad_normed - normed * jnp.mean(grad_normed * normed, axis=-1, keepdims=True))


def rotate(values, cos_part, sin_part):
    half_size = values.shape[-1] // 2
    turned = jnp.concatenate([-values[..., half_size:], values[..., :half_size]], axis=-1)
    return values * cos_part + turned * sin_part


def rotate_back(grads, cos_part, sin_part):
    half_size = grads.shape[-1] // 2
    scaled = grads * sin_part
    return grads * cos_part + jnp.concatenate(
        [scaled[..., half_size:], -scaled[..., :half_size]], axis=-1
    )


def round_trip(values):
    return lax.optimization_barrier(values.astype(jnp.bfloat16)).astype(jnp.float32)


def shards(tokens, w_attn, w_mlp, norm_gains, qk_gains, cotangent):
    seq_count, block_len, model_width = tokens.shape
    row_count = seq_count * block_len
    seq_index = lax.axis_index("seq")
    reach_count = min(-(-(WINDOW - 1) // block_len), lax.axis_size("seq") - 1)
    q_width = HEADS * HEAD
    split_qkv = q_width + 2 * HEAD
    inputs = tokens.reshape(row_count, model_width).astype(jnp.float32)
    grad_out = cotangent.reshape(row_count, model_width).astype(jnp.float32)
    attn_full, gains_full, qk_full = (
        lax.all_gather(w_attn, "fsdp", axis=0, tiled=True),
        lax.all_gather(norm_gains, "fsdp", axis=1, tiled=True),
        lax.all_gather(qk_gains, "fsdp", axis=1, tiled=True),
    )
    norm_gain = gains_full.astype(jnp.float32)
    qk_gain = qk_full.astype(jnp.float32)
    positions = (seq_index * block_len + jnp.arange(block_len, dtype=jnp.int32)).astype(jnp.float32)
    half_size = HEAD // 2
    frequency = ROPE_BASE ** (-(jnp.arange(half_size, dtype=jnp.float32) * 2.0) / HEAD)
    angles = positions[:, None] * frequency[None, :]
    cos_table = jnp.concatenate([jnp.cos(angles), jnp.cos(angles)], axis=-1)
    sin_table = jnp.concatenate([jnp.sin(angles), jnp.sin(angles)], axis=-1)
    cos_q = cos_table[None, :, None, :]
    sin_q = sin_table[None, :, None, :]
    cos_k = cos_table[None]
    sin_k = sin_table[None]
    inv_in = inverse_rms(inputs)
    normed_in = inputs * inv_in
    hidden_in = (normed_in * norm_gain[0]).astype(jnp.bfloat16)
    project = jnp.dot(hidden_in, attn_full[:, :split_qkv], preferred_element_type=jnp.float32)
    q_raw = project[:, :q_width].reshape(seq_count, block_len, HEADS, HEAD)
    k_raw = project[:, q_width : q_width + HEAD].reshape(seq_count, block_len, HEAD)
    v_low = project[:, q_width + HEAD :].astype(jnp.bfloat16).reshape(seq_count, block_len, HEAD)
    inv_q = inverse_rms(q_raw)
    normed_q = q_raw * inv_q
    inv_k = inverse_rms(k_raw)
    normed_k = k_raw * inv_k
    q_low = (rotate(normed_q * qk_gain[0], cos_q, sin_q) * HEAD ** (-0.5)).astype(jnp.bfloat16)
    k_low = rotate(normed_k * qk_gain[1], cos_k, sin_k).astype(jnp.bfloat16)
    key_parts = []
    value_parts = []
    for offset in range(reach_count, 0, -1):
        moved_k, moved_v = passed_along((k_low, v_low), "seq", offset)
        key_parts.append(moved_k)
        value_parts.append(moved_v)
    key_all = jnp.concatenate(key_parts + [k_low], axis=1)
    value_all = jnp.concatenate(value_parts + [v_low], axis=1)
    key_span = (reach_count + 1) * block_len
    row_pos = jnp.arange(block_len, dtype=jnp.int32)[:, None]
    col_pos = jnp.arange(key_span, dtype=jnp.int32)[None, :]
    distance = reach_count * block_len + row_pos - col_pos
    allowed = (
        (distance >= 0)
        & (distance < WINDOW)
        & ((seq_index - reach_count) * block_len + col_pos >= 0)
    )

    def scores_of():
        raw_scores = jnp.einsum(
            "sbhc,stc->shbt", q_low, key_all, preferred_element_type=jnp.float32
        )
        return jnp.where(allowed[None, None], raw_scores, MASKED)

    scores = scores_of()
    row_top = jnp.max(scores, axis=-1, keepdims=True)
    exponent = jnp.exp(scores - row_top)
    denominator = jnp.sum(exponent, axis=-1, keepdims=True)
    log_total = row_top + jnp.log(denominator)
    attn_probs = exponent / denominator
    attn_out = jnp.einsum(
        "shbt,stc->sbhc",
        attn_probs.astype(jnp.bfloat16),
        value_all,
        preferred_element_type=jnp.float32,
    )
    mixed_low = attn_out.reshape(row_count, q_width).astype(jnp.bfloat16)
    branch = jnp.einsum(
        "nk,dk->nd", mixed_low, attn_full[:, split_qkv:], preferred_element_type=jnp.float32
    )
    inv_a = inverse_rms(branch)
    normed_a = branch * inv_a
    middle = inputs + normed_a * norm_gain[1]
    mlp_full = lax.all_gather(w_mlp, "fsdp", axis=0, tiled=True)
    inv_mid = inverse_rms(middle)
    normed_mid = middle * inv_mid
    hidden_ff = (normed_mid * norm_gain[2]).astype(jnp.bfloat16)
    gate_up = jnp.dot(hidden_ff, mlp_full[:, : 2 * FF], preferred_element_type=jnp.float32)
    gate_out = gate_up[:, :FF]
    up_out = gate_up[:, FF:]
    gelu_out, gelu_pull = jax.vjp(partial(jax.nn.gelu, approximate=True), gate_out)
    product_low = (gelu_out * up_out).astype(jnp.bfloat16)
    branch_ff = jnp.einsum(
        "nf,df->nd", product_low, mlp_full[:, 2 * FF :], preferred_element_type=jnp.float32
    )
    inv_ff = inverse_rms(branch_ff)
    normed_ff = branch_ff * inv_ff
    result = (middle + normed_ff * norm_gain[3]).astype(jnp.bfloat16).reshape(tokens.shape)
    mlp_back = lax.all_gather(w_mlp, "fsdp", axis=0, tiled=True)
    attn_back = lax.all_gather(w_attn, "fsdp", axis=0, tiled=True)
    grad_gain_po = jnp.sum(grad_out * normed_ff, axis=0)
    down_low = rms_back(grad_out * norm_gain[3], normed_ff, inv_ff).astype(jnp.bfloat16)
    grad_product = jnp.dot(down_low, mlp_back[:, 2 * FF :], preferred_element_type=jnp.float32)
    grad_gate = gelu_pull(grad_product * up_out)[0]
    grad_up = grad_product * gelu_out
    gu_low = jnp.concatenate([grad_gate, grad_up], axis=1).astype(jnp.bfloat16)
    grad_hidden_ff = jnp.einsum(
        "nf,df->nd", gu_low, mlp_back[:, : 2 * FF], preferred_element_type=jnp.float32
    )
    grad_gain_pf = jnp.sum(grad_hidden_ff * normed_mid, axis=0)
    grad_middle = grad_out + rms_back(grad_hidden_ff * norm_gain[2], normed_mid, inv_mid)
    left_down = lax.slice_in_dim(down_low, 0, w_mlp.shape[0] * lax.axis_size("fsdp"), axis=1)
    upper_part = jnp.einsum("nd,nf->df", hidden_ff, gu_low, preferred_element_type=jnp.float32)
    lower_part = jnp.einsum("nd,nf->df", left_down, product_low, preferred_element_type=jnp.float32)
    mlp_grad = lax.psum_scatter(
        jnp.concatenate([upper_part, lower_part], axis=1).astype(jnp.bfloat16),
        "fsdp",
        scatter_dimension=0,
        tiled=True,
    )
    grad_gain_pa = jnp.sum(grad_middle * normed_a, axis=0)
    branch_low = rms_back(grad_middle * norm_gain[1], normed_a, inv_a).astype(jnp.bfloat16)
    grad_wo = jnp.einsum("nd,nk->dk", branch_low, mixed_low, preferred_element_type=jnp.float32)
    grad_mixed = jnp.dot(branch_low, attn_back[:, split_qkv:], preferred_element_type=jnp.float32)
    mixed_grad_low = grad_mixed.astype(jnp.bfloat16).reshape(seq_count, block_len, HEADS, HEAD)
    probs_again = jnp.exp(scores_of() - log_total)
    grad_values_all = jnp.einsum(
        "shbt,sbhc->stc",
        probs_again.astype(jnp.bfloat16),
        mixed_grad_low,
        preferred_element_type=jnp.float32,
    )
    grad_probs = jnp.einsum(
        "sbhc,stc->shbt", mixed_grad_low, value_all, preferred_element_type=jnp.float32
    )
    row_delta = jnp.sum(probs_again * grad_probs, axis=-1, keepdims=True)
    score_grad = (probs_again * (grad_probs - row_delta)).astype(jnp.bfloat16)
    grad_q = jnp.einsum("shbt,stc->sbhc", score_grad, key_all, preferred_element_type=jnp.float32)
    grad_keys_all = jnp.einsum(
        "shbt,sbhc->stc", score_grad, q_low, preferred_element_type=jnp.float32
    )
    grad_keys = grad_keys_all[:, reach_count * block_len :]
    grad_vals = grad_values_all[:, reach_count * block_len :]
    for offset in range(reach_count, 0, -1):
        first_col = (reach_count - offset) * block_len
        back_k, back_v = (
            passed_along(
                grad_keys_all[:, first_col : first_col + block_len].astype(jnp.bfloat16),
                "seq",
                -offset,
            ).astype(jnp.float32),
            passed_along(
                grad_values_all[:, first_col : first_col + block_len].astype(jnp.bfloat16),
                "seq",
                -offset,
            ).astype(jnp.float32),
        )
        grad_keys = grad_keys + back_k
        grad_vals = grad_vals + back_v
    grad_qs = rotate_back(round_trip(grad_q) * HEAD ** (-0.5), cos_q, sin_q)
    grad_qk_q = jnp.sum(grad_qs * normed_q, axis=(0, 1, 2))
    grad_q_raw = rms_back(grad_qs * qk_gain[0], normed_q, inv_q)
    grad_ks = rotate_back(round_trip(grad_keys), cos_k, sin_k)
    grad_qk_k = jnp.sum(grad_ks * normed_k, axis=(0, 1))
    grad_k_raw = rms_back(grad_ks * qk_gain[1], normed_k, inv_k)
    proj_low = jnp.concatenate(
        [
            grad_q_raw.reshape(row_count, q_width),
            grad_k_raw.reshape(row_count, HEAD),
            grad_vals.reshape(row_count, HEAD),
        ],
        axis=1,
    ).astype(jnp.bfloat16)
    grad_qkv = jnp.einsum("nd,nk->dk", hidden_in, proj_low, preferred_element_type=jnp.float32)
    grad_hidden_in = jnp.einsum(
        "nk,dk->nd", proj_low, attn_back[:, :split_qkv], preferred_element_type=jnp.float32
    )
    grad_gain_in = jnp.sum(grad_hidden_in * normed_in, axis=0)
    grad_inputs = grad_middle + rms_back(grad_hidden_in * norm_gain[0], normed_in, inv_in)
    attn_grad_full = jnp.concatenate([grad_qkv, grad_wo], axis=1)
    gain_grad_full = jnp.stack([grad_gain_in, grad_gain_pa, grad_gain_pf, grad_gain_po])
    qk_grad_full = jnp.stack([grad_qk_q, grad_qk_k])
    attn_part, gain_part, qk_part = (
        lax.psum_scatter(
            attn_grad_full.astype(jnp.bfloat16), "fsdp", scatter_dimension=0, tiled=True
        ).astype(jnp.float32),
        lax.psum_scatter(
            gain_grad_full.astype(jnp.bfloat16), "fsdp", scatter_dimension=1, tiled=True
        ).astype(jnp.float32),
        lax.psum_scatter(
            qk_grad_full.astype(jnp.bfloat16), "fsdp", scatter_dimension=1, tiled=True
        ).astype(jnp.float32),
    )
    attn_total, mlp_total, gain_total, qk_total = (
        lax.psum(attn_part.astype(jnp.bfloat16), "seq").astype(jnp.float32),
        lax.psum(mlp_grad, "seq").astype(jnp.float32),
        lax.psum(gain_part.astype(jnp.bfloat16), "seq").astype(jnp.float32),
        lax.psum(qk_part.astype(jnp.bfloat16), "seq").astype(jnp.float32),
    )
    return (result, grad_inputs.reshape(tokens.shape), attn_total, mlp_total, gain_total, qk_total)


def solution(mesh):
    in_specs = (
        P("fsdp", "seq", None),
        P("fsdp", None),
        P("fsdp", None),
        P(None, "fsdp"),
        P(None, "fsdp"),
        P("fsdp", "seq", None),
    )
    out_specs = (
        P("fsdp", "seq", None),
        P("fsdp", "seq", None),
        P("fsdp", None),
        P("fsdp", None),
        P(None, "fsdp"),
        P(None, "fsdp"),
    )
    return jax.shard_map(shards, mesh=mesh, in_specs=in_specs, out_specs=out_specs, check_vma=False)
```

profile of v0, /device:TPU:16, one launch (start us, length us, event | category | flops | bytes accessed | tf_op | source)
XLA Modules:
  0.0 1084.1 jit_solution(10114522160547290943)
XLA Ops:
  8.7 20.7 %all-gather.1 = bf16[16,16,2]{1,2,0:T(2,128)(2,1)S(1)} all-gather(bf16[1,16,2]{1,2,0:T(2,128)(2,1)} %bitcast.194), channel_id=1, replica_groups=mesh['seq'=8,'fsdp'=16] {'fsdp'}, dimensions={0}, use_global_device_ids=true | all-gather | bytes 1088 | tf_op jit(solution)/shard_map/all_gather | solution.py:63
  30.1 24.5 %all-gather = bf16[16,72,4]{1,2,0:T(4,128)(2,1)S(1)} all-gather(bf16[1,72,4]{1,2,0:T(4,128)(2,1)} %bitcast.193), channel_id=1, replica_groups=mesh['seq'=8,'fsdp'=16] {'fsdp'}, dimensions={0}, use_global_device_ids=true | all-gather | bytes 9792 | tf_op jit(solution)/shard_map/all_gather | solution.py:62
  56.1 16.8 %all-gather.5.cloned.1.call-done = bf16[1152,2560]{1,0:T(8,128)(2,1)} async-done(((bf16[72,2560]{1,0:T(8,128)(2,1)}), bf16[1152,2560]{1,0:T(8,128)(2,1)}) %all-gather.5.cloned.1.call-update) | async-done | bytes 5898256 | tf_op jit(solution)/shard_map/all_gather | solution.py:61
  72.8 2.7 fusion.17
  76.3 4.6 collective-permute-start.3
  80.9 3.4 collective-permute-start.2
  84.3 3.4 collective-permute-start.1
  87.6 3.2 collective-permute-start
  110.3 6.3 collective-permute-start.7
  116.6 3.4 collective-permute-done.7
  127.5 2.7 multiply_reduce_fusion.7
  130.8 196.6 %all-gather.7.cloned.1.call-done = bf16[1152,20736]{1,0:T(8,128)(2,1)} async-done(((bf16[72,20736]{1,0:T(8,128)(2,1)}), bf16[1152,20736]{1,0:T(8,128)(2,1)}) %all-gather.7.cloned.1.call-update) | async-done | bytes 47775760 | tf_op jit(solution)/shard_map/all_gather | solution.py:133
  327.4 15.6 %fusion.2 = f32[128,13824]{1,0:T(8,128)} fusion(bf16[1152,20736]{1,0:T(8,128)(2,1)} %all-gather.7.cloned.1.call-done, f32[128,1152]{1,0:T(8,128)S(1)} %get-tuple-element.28, f32[1152]{0:T(1024)S(1)} %get-tuple-element.19, f32[128]{0:T(128)S(1)} %add_rsqrt_fusion.2), kind=kOutput, calls=%fused_computation.4 | convolution fusion | flops 4077305856 | bytes 39523328 | tf_op jit(solution)/shard_map/dot_general | solution.py:137
  343.0 4.3 multiply_convert_fusion.1
  347.3 9.2 multiply_reduce_fusion.5
  358.4 11.1 %fusion.14 = (bf16[128,6912]{1,0:T(8,128)(2,1)}, bf16[128,6912]{1,0:T(8,128)(2,1)}) fusion(f32[128,13824]{1,0:T(8,128)} %fusion.2, bf16[128,1152]{1,0:T(8,128)(2,1)S(1)} %get-tuple-element.31, bf16[1152,20736]{1,0:T(8,128)(2,1)} %all-gather.7.cloned.1.call-done), kind=kOutput, calls=%fused_computation.22 | convolution fusion | flops 2059665408 | bytes 26836992 | tf_op jit(solution)/shard_map/dot_general | solution.py:152
  369.4 16.2 %multiply_reduce_fusion.1 = (bf16[1152]{0:T(1024)(128)(2,1)}, f32[128]{0:T(128)S(1)}, f32[128,1152]{1,0:T(8,128)S(1)}) fusion(f32[128,1152]{1,0:T(8,128)S(1)} %get-tuple-element.28, f32[128]{0:T(128)S(1)} %add_rsqrt_fusion.2, f32[1152]{0:T(1024)S(1)} %get-tuple-element.19, bf16[1152,20736]{1,0:T(8,128)(2,1)} %all-gather.7.cloned.1.call-done, ...), kind=kOutput, calls=%fused_computation.81 | convolution fusion | flops 4084825088 | bytes 36577024 | tf_op jit(solution)/shard_map/nf,df->nd/dot_general | solution.py:156
  388.3 2.9 fusion.24
  397.4 7.9 convolution_convert_fusion.1
  423.9 3.0 collective-permute-done.14
  426.9 3.4 collective-permute-done.13
  433.5 3.0 pad_maximum_fusion.1
  437.9 16.3 %convolution_convert_fusion = bf16[1152,13824]{1,0:T(8,128)(2,1)} fusion(bf16[128,6912]{1,0:T(8,128)(2,1)} %get-tuple-element.30, bf16[128,6912]{1,0:T(8,128)(2,1)S(1)} %copy-done.12, f32[128,1152]{1,0:T(8,128)S(1)} %get-tuple-element.28, f32[1152]{0:T(1024)S(1)} %get-tuple-element.19, f32[128]{0:T(128)S(1)} %copy-done.30), kind=kOutput, calls=%fused_computation | convolution fusion | flops 4100308992 | bytes 35984384 | tf_op jit(solution)/shard_map/nd,nf->df/dot_general | solution.py:162
  454.3 32.9 %pad_maximum_fusion = bf16[1152,20736]{1,0:T(8,128)(2,1)} fusion(bf16[1152,6912]{1,0:T(8,128)(2,1)} %convolution_convert_fusion.1, bf16[1152,13824]{1,0:T(8,128)(2,1)} %convolution_convert_fusion), kind=kLoop, calls=%fused_computation.1 | loop fusion | flops 95551488 | bytes 95551488 | tf_op jit(solution)/shard_map/concatenate | solution.py:165
  488.7 34.2 %reduce-scatter.7.cloned.1.call-done = bf16[72,2560]{1,0:T(8,128)(2,1)} async-done(((bf16[1152,2560]{1,0:T(8,128)(2,1)}), bf16[72,2560]{1,0:T(8,128)(2,1)}) %reduce-scatter.7.cloned.1.call-update) | async-done | bytes 368656 | tf_op jit(solution)/shard_map/reduce_scatter | solution.py:233
  522.9 325.7 %reduce-scatter.9.cloned.1.call-done = bf16[72,20736]{1,0:T(8,128)(2,1)} async-done(((bf16[1152,20736]{1,0:T(8,128)(2,1)}), bf16[72,20736]{1,0:T(8,128)(2,1)}) %reduce-scatter.9.cloned.1.call-update) | async-done | bytes 2986000 | tf_op jit(solution)/shard_map/reduce_scatter | solution.py:164
  849.9 3.4 fusion.50
  853.3 31.5 %all-reduce = bf16[4,1152]{1,0:T(4,128)(2,1)S(1)} all-reduce(bf16[4,1152]{1,0:T(4,128)(2,1)S(1)} %pad_maximum_fusion.10), channel_id=4, replica_groups=mesh['seq'=8,'fsdp'=16] {'fsdp'}, use_global_device_ids=true, to_apply=%region_23.24.clone | all-reduce | flops 4608 | bytes 18432
  885.9 29.0 %reduce-scatter.11.cloned.1.call-done = bf16[16,2]{1,0:T(8,128)(2,1)} async-done(((bf16[256,2]{1,0:T(8,128)(2,1)}), bf16[16,2]{1,0:T(8,128)(2,1)}) %reduce-scatter.11.cloned.1.call-update) | async-done | bytes 80
  915.7 21.0 %all-reduce.1 = (bf16[4,72]{1,0:T(4,128)(2,1)S(1)}, bf16[2,16]{1,0:T(2,128)(2,1)S(1)}) all-reduce(bf16[4,72]{1,0:T(4,128)(2,1)S(1)} %constant_dynamic-slice_fusion, bf16[2,16]{1,0:T(2,128)(2,1)S(1)} %copy.143), channel_id=1, replica_groups=mesh['seq'=8,'fsdp'=16] {'seq'}, use_global_device_ids=true, to_apply=%region_24.25 | all-reduce | flops 320 | bytes 1280 | tf_op jit(solution)/shard_map/psum | solution.py:246
  937.9 132.6 %all-reduce.5.cloned.1.call-done = (bf16[72,2560]{1,0:T(8,128)(2,1)}, bf16[72,20736]{1,0:T(8,128)(2,1)}) async-done(((bf16[72,2560]{1,0:T(8,128)(2,1)}, bf16[72,20736]{1,0:T(8,128)(2,1)}), (bf16[72,2560]{1,0:T(8,128)(2,1)}, bf16[72,20736]{1,0:T(8,128)(2,1)})) %all-reduce.5.cloned.1.call-update) | async-done | bytes 3354640 | tf_op jit(solution)/shard_map/psum | solution.py:244
  1072.4 4.8 convert_element_type.201
  (237 shorter events, 72.2 us)
Async XLA Ops:
  7.2 65.7 %all-gather.5.cloned.1.call-start = ((), (), s32[]{:S(2)}) async-start(), calls=%async_computation.3 | async-start | bytes 6266880 | tf_op jit(solution)/shard_map/all_gather | solution.py:61
  7.9 319.5 %all-gather.7.cloned.1.call-start = ((), (), s32[]{:S(2)}) async-start(), calls=%async_computation.4 | async-start | bytes 50761728 | tf_op jit(solution)/shard_map/all_gather | solution.py:133
  8.7 514.2 %reduce-scatter.7.cloned.1.call-start = ((), (), s32[]{:S(2)}) async-start(), calls=%async_computation.5 | async-start | bytes 6266880 | tf_op jit(solution)/shard_map/reduce_scatter | solution.py:233
  29.5 65.3 %copy-start.31 = (f32[1,256]{1,0:T(1,128)}, f32[1,256]{1,0:T(1,128)S(1)}, u32[]{:S(2)}) copy-start(f32[1,256]{1,0:T(1,128)S(1)} %get-tuple-element.54) | copy-start | bytes 3076
  76.3 47.3 %collective-permute-start.3 = (bf16[1,128,256]{2,1,0:T(8,128)(2,1)}, bf16[1,128,256]{2,1,0:T(8,128)(2,1)}, u32[]{:S(2)}, u32[]{:S(2)}) collective-permute-start(bf16[1,128,256]{2,1,0:T(8,128)(2,1)} %fusion.88), channel_id=1, source_target_pairs={{0,16},{16,32},{32,48},{48,64},{64,80},{80,96},{96,112},{1,17},{17... | collective-permute-start | bytes 196616 | tf_op jit(solution)/shard_map/ppermute | solution.py:22
  80.9 41.8 %collective-permute-start.2 = (bf16[1,128,256]{2,1,0:T(8,128)(2,1)}, bf16[1,128,256]{2,1,0:T(8,128)(2,1)}, u32[]{:S(2)}, u32[]{:S(2)}) collective-permute-start(bf16[1,128,256]{2,1,0:T(8,128)(2,1)} %fusion.88), channel_id=1, source_target_pairs={{0,32},{16,48},{32,64},{48,80},{64,96},{80,112},{1,33},{17,49},{33... | collective-permute-start | bytes 196616 | tf_op jit(solution)/shard_map/ppermute | solution.py:22
  84.3 37.6 %collective-permute-start.1 = (bf16[1,128,256]{2,1,0:T(8,128)(2,1)}, bf16[1,128,256]{2,1,0:T(8,128)(2,1)}, u32[]{:S(2)}, u32[]{:S(2)}) collective-permute-start(bf16[1,128,256]{2,1,0:T(8,128)(2,1)} %fusion.88), channel_id=1, source_target_pairs={{0,48},{16,64},{32,80},{48,96},{64,112},{1,49},{17,65},{33,81},{49... | collective-permute-start | bytes 196616 | tf_op jit(solution)/shard_map/ppermute | solution.py:22
  87.6 33.3 %collective-permute-start = (bf16[1,128,256]{2,1,0:T(8,128)(2,1)}, bf16[1,128,256]{2,1,0:T(8,128)(2,1)}, u32[]{:S(2)}, u32[]{:S(2)}) collective-permute-start(bf16[1,128,256]{2,1,0:T(8,128)(2,1)} %fusion.88), channel_id=1, source_target_pairs={{0,64},{16,80},{32,96},{48,112},{1,65},{17,81},{33,97},{49,113},{2... | collective-permute-start | bytes 196616 | tf_op jit(solution)/shard_map/ppermute | solution.py:22
  91.9 11.4 %collective-permute-start.4 = (bf16[1,128,256]{2,1,0:T(8,128)(2,1)}, bf16[1,128,256]{2,1,0:T(8,128)(2,1)}, u32[]{:S(2)}, u32[]{:S(2)}) collective-permute-start(bf16[1,128,256]{2,1,0:T(8,128)(2,1)} %get-tuple-element.50), channel_id=1, source_target_pairs={{0,64},{16,80},{32,96},{48,112},{1,65},{17,81},{33,97},{49,113},{2... | collective-permute-start | bytes 196616 | tf_op jit(solution)/shard_map/ppermute | solution.py:22
  103.3 3.5 collective-permute-start.5
  106.8 3.5 collective-permute-start.6
  110.3 9.8 collective-permute-start.7
  130.8 254.8 %copy-start.29 = (f32[128]{0:T(128)}, f32[128]{0:T(128)S(1)}, u32[]{:S(2)}) copy-start(f32[128]{0:T(128)S(1)} %add_rsqrt_fusion.2) | copy-start | bytes 1540
  406.0 17.9 %collective-permute-start.12 = (bf16[1,128,256]{1,2,0:T(8,128)(2,1)}, bf16[1,128,256]{1,2,0:T(8,128)(2,1)}, u32[]{:S(2)}, u32[]{:S(2)}) collective-permute-start(bf16[1,128,256]{1,2,0:T(8,128)(2,1)} %get-tuple-element.41), channel_id=1, source_target_pairs={{64,0},{80,16},{96,32},{112,48},{65,1},{81,17},{97,33},{113,49},{6... | collective-permute-start | bytes 196616 | tf_op jit(solution)/shard_map/ppermute | solution.py:22
  408.7 8.3 collective-permute-start.8
  410.0 8.3 collective-permute-start.11
  411.3 8.3 collective-permute-start.10
  412.6 8.9 collective-permute-start.9
  416.9 7.0 collective-permute-start.15
  418.2 8.7 collective-permute-start.14
  419.6 10.7 collective-permute-start.13
  436.5 412.0 %reduce-scatter.9.cloned.1.call-start = ((), (), s32[]{:S(2)}) async-start(), calls=%async_computation.6 | async-start | bytes 50761728 | tf_op jit(solution)/shard_map/reduce_scatter | solution.py:164
  487.2 361.4 %copy-start.46 = (u32[128]{0:T(128)S(1)}, u32[128]{0:T(128)}, u32[]{:S(2)}) copy-start(u32[128]{0:T(128)} %constant.71) | copy-start | bytes 1540
  487.2 362.6 %copy-start.35 = (bf16[1152]{0:T(1024)(128)(2,1)S(1)}, bf16[1152]{0:T(1024)(128)(2,1)}, u32[]{:S(2)}) copy-start(bf16[1152]{0:T(1024)(128)(2,1)} %get-tuple-element.16) | copy-start | bytes 6916
  487.2 362.6 %copy-start.42 = (bf16[1152]{0:T(1024)(128)(2,1)S(1)}, bf16[1152]{0:T(1024)(128)(2,1)}, u32[]{:S(2)}) copy-start(bf16[1152]{0:T(1024)(128)(2,1)} %get-tuple-element.10) | copy-start | bytes 6916
  487.3 362.6 %copy-start.36 = (bf16[1152]{0:T(1024)(128)(2,1)S(1)}, bf16[1152]{0:T(1024)(128)(2,1)}, u32[]{:S(2)}) copy-start(bf16[1152]{0:T(1024)(128)(2,1)} %get-tuple-element.8) | copy-start | bytes 6916
  487.3 362.6 %copy-start.6 = (bf16[1,128,1152]{2,1,0:T(8,128)(2,1)S(1)}, bf16[1,128,1152]{2,1,0:T(8,128)(2,1)}, u32[]{:S(2)}) copy-start(bf16[1,128,1152]{2,1,0:T(8,128)(2,1)} %param.6) | copy-start | bytes 884740
  487.3 362.6 %copy-start.20 = (bf16[1,128,4,256]{1,3,2,0:T(8,128)(2,1)S(1)}, bf16[1,128,4,256]{1,3,2,0:T(8,128)(2,1)}, u32[]{:S(2)}) copy-start(bf16[1,128,4,256]{1,3,2,0:T(8,128)(2,1)} %multiply_convert_fusion.6) | copy-start | bytes 786436
  487.3 362.6 %copy-start.26 = (bf16[128,256]{0,1:T(8,128)(2,1)S(1)}, bf16[128,256]{0,1:T(8,128)(2,1)}, u32[]{:S(2)}) copy-start(bf16[128,256]{0,1:T(8,128)(2,1)} %copy-done.25) | copy-start | bytes 196612
  487.3 362.6 %copy-start.44 = (f32[128]{0:T(128)S(1)}, f32[128]{0:T(128)}, u32[]{:S(2)}) copy-start(f32[128]{0:T(128)} %copy-done.43) | copy-start | bytes 1540
  487.3 427.7 %reduce-scatter.11.cloned.1.call-start = ((), (), s32[]{:S(2)}) async-start(), calls=%async_computation.7 | async-start | bytes 69632
  488.6 581.9 %all-reduce.5.cloned.1.call-start = ((), (), s32[]{:S(2)}) async-start(), calls=%async_computation.8 | async-start | bytes 6709248 | tf_op jit(solution)/shard_map/psum | solution.py:244
  (37 other events, 412.9 us)
Sparse Core Ops, SparseCore 0:
  10.5 62.3 all-gather.4
  75.2 252.1 all-gather.6
  436.6 86.2 reduce-scatter.6
  527.9 320.5 reduce-scatter.8
  852.9 61.9 reduce-scatter.10
  917.4 153.0 all-reduce.4
where the time goes:
time: 1090 us; the launch traced here: 1080 us
  waiting for transfers between devices  752 us (69%)
  matrix products  97.8 us (9%)
  blocking collectives  97.6 us (9%)
  other arithmetic  62 us (6%)
  starting transfers between devices  35.9 us (3%)
  local copies, waits for them, and re-layouts  23.4 us (2%)
  between operations  15.8 us (1%)
    reduce_scatter x1, waiting for transfers between devices, shards(): lax.psum_scatter(jnp.concatenate([upper_part, lower_part], axis=1).astype...  326 us
    all_gather x1, waiting for transfers between devices, shards(): mlp_full = lax.all_gather(w_mlp, 'fsdp', axis=0, tiled=True)  197 us
    psum x1, waiting for transfers between devices, shards(): lax.psum(attn_part.astype(jnp.bfloat16), 'seq').astype(jnp.float32)  133 us
    ppermute x16, starting transfers between devices, passed_along(): lax.ppermute(value, axis, [(source, source + steps) for source in range(i...  35.6 us
    reduce_scatter x1, waiting for transfers between devices, shards(): lax.psum_scatter(attn_grad_full.astype(jnp.bfloat16), 'fsdp', scatter_dim...  34.2 us
    concatenate x1, other arithmetic, shards(): jnp.concatenate([upper_part, lower_part], axis=1).astype(jnp.bfloat16)  32.9 us
    unnamed x1, blocking collectives  31.5 us
    unnamed x7, waiting for transfers between devices  30.5 us
  transfers between devices with their start and end apart: 22, of which 14 were waited for; matrix products, arithmetic and copies ran while one was open for 8% of the time, Pallas kernels for 0%

commit v1 on v0

v1 whole, which is shorter than its diff:
```python
from functools import partial

import jax
import jax.numpy as jnp
from jax import lax
from jax.experimental import pallas as pl
from jax.experimental.pallas import tpu as pltpu
from jax.sharding import Mesh
from jax.sharding import PartitionSpec as P

HEADS = 4
HEAD = 256
FF = 6912
WINDOW = 512


EPSILON = 1e-06
ROPE_BASE = 10000.0
MASKED = -1e30


def inverse_rms(values):
    return lax.rsqrt(jnp.mean(values * values, axis=-1, keepdims=True) + EPSILON)


MESH = pl.DeviceIdType.MESH
LANES = 128
ROWS = 128
CHIPS = 4


def vmem_spec():
    return pl.BlockSpec(memory_space=pltpu.VMEM)


def nt_dot(left, right):
    return lax.dot_general(
        left, right, (((1,), (1,)), ((), ())), preferred_element_type=jnp.float32
    )


def meet(peers):
    barrier = pltpu.get_barrier_semaphore()
    for peer in peers:
        pl.semaphore_signal(barrier, inc=1, device_id=peer, device_id_type=MESH)
    pl.semaphore_wait(barrier, len(peers))


def group_peers():
    chip, core = lax.axis_index("x"), lax.axis_index("c")
    sibling = {"c": 1 - core}
    right = {"x": lax.rem(chip + 1, CHIPS)}
    left = {"x": lax.rem(chip + CHIPS - 1, CHIPS)}
    return sibling, right, left


def rows_of(chip_step, core_step, first=0, count=ROWS):
    return pl.ds((chip_step * 2 + core_step) * ROWS + first, count)


def exchange_stage(blocks, partial, sib_in, outgoing, inbox, transit, sends, recvs, chunk, filler):
    sibling, right, left = group_peers()
    half = ROWS // 2

    def copy(number, source, target, peer):
        return pltpu.make_async_remote_copy(
            src_ref=source,
            dst_ref=target,
            send_sem=sends.at[number],
            recv_sem=recvs.at[number],
            device_id=peer,
            device_id_type=MESH,
        )

    own = blocks.at[rows_of(0, 0)]
    started = []

    def start(*args):
        made = copy(*args)
        made.start()
        started.append(made)
        return made

    to_right = start(0, own, blocks.at[rows_of(3, 0)], right)
    to_left = start(1, own, blocks.at[rows_of(1, 0)], left)
    to_sib = start(2, own, blocks.at[rows_of(0, 1)], sibling)

    def run(step):
        partial[pl.ds(step * 2 * ROWS, 2 * ROWS), :] = chunk(step)
        outgoing[rows_of(step, 1), :] = partial[rows_of(step, 1), :].astype(jnp.bfloat16)
        return start(
            8 + step, outgoing.at[rows_of(step, 1)], sib_in.at[pl.ds(step * ROWS, ROWS)], sibling
        )

    def paired(step, given):
        given.wait_recv()
        both = partial[rows_of(step, 0), :] + sib_in[pl.ds(step * ROWS, ROWS), :].astype(
            jnp.float32
        )
        outgoing[rows_of(step, 0), :] = both.astype(jnp.bfloat16)

    to_sib.wait_recv()
    sib_0 = run(0)
    to_right.wait_recv()
    share_3 = start(3, blocks.at[rows_of(3, 0)], blocks.at[rows_of(3, 1)], sibling)
    far_right = start(
        4, blocks.at[rows_of(3, 0, 0, half)], blocks.at[rows_of(2, 0, 0, half)], right
    )
    to_left.wait_recv()
    share_1 = start(5, blocks.at[rows_of(1, 0)], blocks.at[rows_of(1, 1)], sibling)
    far_left = start(
        6, blocks.at[rows_of(1, 0, half, half)], blocks.at[rows_of(2, 0, half, half)], left
    )
    share_3.wait_recv()
    sib_3 = run(3)
    far_right.wait_recv()
    far_left.wait_recv()
    share_2 = start(7, blocks.at[rows_of(2, 0)], blocks.at[rows_of(2, 1)], sibling)
    paired(3, sib_3)
    sum_left = start(12, outgoing.at[rows_of(3, 0)], inbox.at[pl.ds(ROWS, ROWS)], left)
    share_1.wait_recv()
    sib_1 = run(1)
    share_2.wait_recv()
    paired(1, sib_1)
    sum_right = start(13, outgoing.at[rows_of(1, 0)], inbox.at[pl.ds(3 * ROWS, ROWS)], right)
    sib_2 = run(2)
    paired(2, sib_2)
    hop_right = start(14, outgoing.at[rows_of(2, 0, 0, half)], transit.at[pl.ds(0, half)], right)
    hop_left = start(15, outgoing.at[rows_of(2, 0, half, half)], transit.at[pl.ds(half, half)], left)
    filler(0)
    hop_right.wait_recv()
    on_right = start(
        16, transit.at[pl.ds(0, half)], inbox.at[pl.ds(2 * ROWS, half)], right
    )
    hop_left.wait_recv()
    on_left = start(
        17, transit.at[pl.ds(half, half)], inbox.at[pl.ds(2 * ROWS + half, half)], left
    )
    filler(1)
    sib_0.wait_recv()
    sum_left.wait_recv()
    sum_right.wait_recv()
    total = partial[rows_of(0, 0), :] + sib_in[pl.ds(0, ROWS), :].astype(jnp.float32)
    total += inbox[pl.ds(ROWS, ROWS), :].astype(jnp.float32)
    total += inbox[pl.ds(3 * ROWS, ROWS), :].astype(jnp.float32)
    on_right.wait_recv()
    on_left.wait_recv()
    total += inbox[pl.ds(2 * ROWS, ROWS), :].astype(jnp.float32)
    for made in started:
        made.wait_send()
    return total


def mlp_kernel(
    hidden_ref,
    middle_ref,
    cot_ref,
    weights_ref,
    gain_ref,
    result_ref,
    grad_hidden_ref,
    gain_grad_ref,
    dw_gu_ref,
    dw_d_ref,
    hidden_all,
    down_all,
    product_all,
    gu_all,
    kept_a,
    kept_b,
    partial,
    sib_in,
    outgoing,
    inbox,
    transit,
    sends,
    recvs,
):
    width = weights_ref.shape[1] // 3
    tiles = width // LANES
    wgu_ref = weights_ref.at[:, pl.ds(0, 2 * width)]
    wd_ref = weights_ref.at[:, pl.ds(2 * width, width)]
    meet(group_peers())
    hidden_all[rows_of(0, 0), :] = hidden_ref[...]
    gelu_scale = 0.7978845608028654

    def forward_chunk(step):
        first = step * 2 * ROWS
        rows = pl.ds(first, 2 * ROWS)

        def tile(index, carry):
            at = pl.multiple_of(index * LANES, LANES)
            both = jnp.dot(
                hidden_all[rows, :],
                wgu_ref[:, pl.ds(pl.multiple_of(2 * at, 2 * LANES), 2 * LANES)],
                preferred_element_type=jnp.float32,
            )
            gate, up = both[:, :LANES], both[:, LANES:]
            square = gate * gate
            turned = jnp.tanh(gelu_scale * gate * (1.0 + 0.044715 * square))
            halved = 0.5 * (1.0 + turned)
            gelu = gate * halved
            slope = halved + 0.5 * gate * (1.0 - turned * turned) * gelu_scale * (
                1.0 + 3 * 0.044715 * square
            )
            product_all[rows, pl.ds(at, LANES)] = (gelu * up).astype(jnp.bfloat16)
            kept_a[rows, pl.ds(at, LANES)] = gelu
            kept_b[rows, pl.ds(at, LANES)] = up * slope
            return carry

        lax.fori_loop(0, tiles, tile, 0)
        return nt_dot(product_all[rows, :], wd_ref[...])

    branch = exchange_stage(
        hidden_all, partial, sib_in.at[0], outgoing.at[0], inbox.at[0], transit.at[0],
        sends.at[0], recvs.at[0], forward_chunk, lambda place: None,
    )
    gain = gain_ref[...]
    grad_out = cot_ref[...].astype(jnp.float32)
    inverse = lax.rsqrt(jnp.mean(branch * branch, axis=-1, keepdims=True) + EPSILON)
    normed = branch * inverse
    result_ref[...] = (middle_ref[...] + normed * gain).astype(jnp.bfloat16)
    gain_grad_ref[...] = jnp.sum(grad_out * normed, axis=0, keepdims=True)
    scaled = grad_out * gain
    down_all[rows_of(0, 0), :] = (
        inverse * (scaled - normed * jnp.mean(scaled * normed, axis=-1, keepdims=True))
    ).astype(jnp.bfloat16)

    def backward_chunk(step):
        first = step * 2 * ROWS
        rows = pl.ds(first, 2 * ROWS)

        for first_tile in range(0, tiles, 2):
            at = first_tile * LANES
            size = min(2 * LANES, width - at)
            grad = jnp.dot(
                down_all[rows, :], wd_ref[:, at : at + size], preferred_element_type=jnp.float32
            )
            gate_grad = low_of(grad * kept_b[rows, at : at + size])
            up_grad = low_of(grad * kept_a[rows, at : at + size])
            for piece in range(0, size, LANES):
                here = 2 * (at + piece)
                gu_all[rows, here : here + LANES] = gate_grad[:, piece : piece + LANES]
                gu_all[rows, here + LANES : here + 2 * LANES] = up_grad[:, piece : piece + LANES]
        return nt_dot(gu_all[rows, :], wgu_ref[...])

    def weight_grads(place):
        if place == 1:
            turned = hidden_all[...].T
            for at in range(0, 2 * width, 256):
                dw_gu_ref[:, at : at + 256] = jnp.dot(
                    turned, gu_all[:, at : at + 256], preferred_element_type=jnp.float32
                ).astype(jnp.bfloat16)
        else:
            turned = down_all[...].T
            for at in range(0, width, 256):
                end = min(at + 256, width)
                dw_d_ref[:, at:end] = jnp.dot(
                    turned, product_all[:, at:end], preferred_element_type=jnp.float32
                ).astype(jnp.bfloat16)

    grad_hidden_ref[...] = exchange_stage(
        down_all, partial, sib_in.at[1], outgoing.at[1], inbox.at[1], transit.at[1],
        sends.at[1], recvs.at[1], backward_chunk, weight_grads,
    )


def mlp_call(hidden, middle, cot, weights, gain):
    rows, model_width = hidden.shape
    width = weights.shape[1] // 3
    group_rows = 2 * CHIPS * rows
    return pl.pallas_call(
        mlp_kernel,
        out_shape=(
            jax.ShapeDtypeStruct((rows, model_width), jnp.bfloat16),
            jax.ShapeDtypeStruct((rows, model_width), jnp.float32),
            jax.ShapeDtypeStruct((1, model_width), jnp.float32),
            jax.ShapeDtypeStruct((model_width, 2 * width), jnp.bfloat16),
            jax.ShapeDtypeStruct((model_width, width), jnp.bfloat16),
        ),
        in_specs=[vmem_spec()] * 5,
        out_specs=tuple([vmem_spec()] * 5),
        scratch_shapes=[
            pltpu.VMEM((group_rows, model_width), jnp.bfloat16),
            pltpu.VMEM((group_rows, model_width), jnp.bfloat16),
            pltpu.VMEM((group_rows, width), jnp.bfloat16),
            pltpu.VMEM((group_rows, 2 * width), jnp.bfloat16),
            pltpu.VMEM((group_rows, width), jnp.float32),
            pltpu.VMEM((group_rows, width), jnp.float32),
            pltpu.VMEM((group_rows, model_width), jnp.float32),
            pltpu.VMEM((2, CHIPS * rows, model_width), jnp.bfloat16),
            pltpu.VMEM((2, group_rows, model_width), jnp.bfloat16),
            pltpu.VMEM((2, CHIPS * rows, model_width), jnp.bfloat16),
            pltpu.VMEM((2, rows, model_width), jnp.bfloat16),
            pltpu.SemaphoreType.DMA((2, 18)),
            pltpu.SemaphoreType.DMA((2, 18)),
        ],
        compiler_params=pltpu.CompilerParams(
            collective_id=0, has_side_effects=True, vmem_limit_bytes=60 * 1024 * 1024
        ),
        cost_estimate=pl.CostEstimate(
            flops=6 * group_rows * model_width * 3 * width, bytes_accessed=20_000_000, transcendentals=0
        ),
        name="feed_forward",
    )(hidden, middle, cot, weights, gain)


def ring_peers(axis):
    place = lax.axis_index(axis)
    return (
        {axis: lax.rem(place + 1, CHIPS)},
        {axis: lax.rem(place + CHIPS - 1, CHIPS)},
        {axis: lax.rem(place + 2, CHIPS)},
    )


def column_peers():
    half, low = lax.axis_index("h"), lax.axis_index("l")
    return ({"h": 1 - half, "l": 1 - low}, {"l": 1 - low}, {"h": 1 - half})


class Copies:
    def __init__(self, sends, recvs):
        self.sends, self.recvs, self.made = sends, recvs, []

    def start(self, source, target, peer):
        number = len(self.made)
        copy = pltpu.make_async_remote_copy(
            src_ref=source,
            dst_ref=target,
            send_sem=self.sends.at[number],
            recv_sem=self.recvs.at[number],
            device_id=peer,
            device_id_type=MESH,
        )
        copy.start()
        self.made.append(copy)
        return copy

    def finish(self):
        for copy in self.made:
            copy.wait_send()


def run_flows(flows):
    waiting = []
    for order, flow in enumerate(flows):
        waiting.append((next(flow), order, flow))
    while waiting:
        waiting.sort(key=lambda entry: entry[:2])
        _, order, flow = waiting.pop(0)
        try:
            waiting.append((next(flow), order, flow))
        except StopIteration:
            pass


def wide(values):
    return values.astype(jnp.float32)


def low_of(values):
    return values.astype(jnp.bfloat16)


def rms_back_of(grad, normed, inverse):
    return inverse * (grad - normed * jnp.mean(grad * normed, axis=-1, keepdims=True))


def turn(values, cos_ref, sin_ref):
    half = HEAD // 2
    first, second = values[:, :half], values[:, half:]
    cos_part, sin_part = cos_ref[...], sin_ref[...]
    return jnp.concatenate(
        [first * cos_part - second * sin_part, second * cos_part + first * sin_part], axis=1
    )


def turn_back(grads, cos_ref, sin_ref):
    half = HEAD // 2
    first, second = grads[:, :half], grads[:, half:]
    cos_part, sin_part = cos_ref[...], sin_ref[...]
    return jnp.concatenate(
        [first * cos_part + second * sin_part, second * cos_part - first * sin_part], axis=1
    )


REACH = 4


def block_peer(step):
    block = lax.rem(lax.axis_index("x") * 2 + lax.axis_index("l") + step + 8, 8)
    return {"x": block // 2, "l": lax.rem(block, 2)}


def flat(values):
    return values.reshape(values.shape[0] * values.shape[1], values.shape[2])


def attention_flow(copies, times, weights, gains_of, tokens_ref, cos_ref, sin_ref, saved):
    gains_ref, qk_ref, raw, q_low, kv_all, probs, mixed, branch_ref, middle_ref, hidden_ref = saved
    seq_block = lax.axis_index("x") * 2 + lax.axis_index("l")
    rows = tokens_ref.shape[0]
    q_width = HEADS * HEAD
    yield times[0]
    gains_of()
    inputs = wide(tokens_ref[...])
    normed = inputs * inverse_rms(inputs)
    hidden_in = low_of(normed * gains_ref[0:1, :])
    for head in range(HEADS + 2):
        at = head * HEAD
        raw_part = jnp.dot(
            hidden_in, flat(weights[:, :, at : at + HEAD]), preferred_element_type=jnp.float32
        )
        if head <= HEADS:
            raw[:, at : at + HEAD] = raw_part
            which = 0 if head < HEADS else 1
            scaled = raw_part * inverse_rms(raw_part) * qk_ref[which : which + 1, :]
            turned = turn(scaled, cos_ref, sin_ref)
            if head < HEADS:
                q_low[:, at : at + HEAD] = low_of(turned * HEAD ** (-0.5))
            else:
                kv_all[REACH, :, :HEAD] = low_of(turned)
        else:
            kv_all[REACH, :, HEAD:] = low_of(raw_part)
    sent = [
        copies.start(kv_all.at[REACH], kv_all.at[REACH - step], block_peer(step))
        for step in range(1, REACH + 1)
    ]
    yield times[1]
    for copy in sent:
        copy.wait_recv()
    span = (REACH + 1) * rows
    row_pos = lax.broadcasted_iota(jnp.int32, (rows, span), 0)
    col_pos = lax.broadcasted_iota(jnp.int32, (rows, span), 1)
    distance = REACH * rows + row_pos - col_pos
    allowed = (
        (distance >= 0) & (distance < WINDOW) & ((seq_block - REACH) * rows + col_pos >= 0)
    )
    keys = flat(kv_all[:, :, :HEAD])
    values = flat(kv_all[:, :, HEAD:])
    for head in range(HEADS):
        at = head * HEAD
        scores = jnp.where(allowed, nt_dot(q_low[:, at : at + HEAD], keys), MASKED)
        exponent = jnp.exp(scores - jnp.max(scores, axis=-1, keepdims=True))
        share = exponent / jnp.sum(exponent, axis=-1, keepdims=True)
        probs[head] = share
        mixed[:, at : at + HEAD] = low_of(
            jnp.dot(low_of(share), values, preferred_element_type=jnp.float32)
        )
    yield times[2]
    branch = nt_dot(mixed[...], flat(weights[:, :, q_width + 2 * HEAD :]))
    branch_ref[...] = branch
    middle = wide(tokens_ref[...]) + branch * inverse_rms(branch) * gains_ref[1:2, :]
    middle_ref[...] = middle
    hidden_ref[...] = low_of(middle * inverse_rms(middle) * gains_ref[2:3, :])


def attention_back_flow(
    copies, times, grad_hidden_ref, po_ref, cot_ref, tokens_ref, weights, cos_ref, sin_ref, saved,
    dwa, small, grad_kv, kv_out, kv_in, grad_q, grad_middle_ref, proj, tokens_grad_ref,
):
    gains_ref, qk_ref, raw, q_low, kv_all, probs, mixed, branch_ref, middle_ref = saved
    q_width = HEADS * HEAD
    split_qkv = q_width + 2 * HEAD
    rows = tokens_ref.shape[0]
    tile = 256
    yield times[0]
    middle = middle_ref[...]
    inverse = inverse_rms(middle)
    normed = middle * inverse
    grad_hidden = grad_hidden_ref[...]
    small[...] = jnp.zeros_like(small)
    small[3:4, :] = po_ref[...]
    small[2:3, :] = jnp.sum(grad_hidden * normed, axis=0, keepdims=True)
    grad_middle = wide(cot_ref[...]) + rms_back_of(grad_hidden * gains_ref[2:3, :], normed, inverse)
    grad_middle_ref[...] = grad_middle
    branch = branch_ref[...]
    inverse = inverse_rms(branch)
    normed = branch * inverse
    small[1:2, :] = jnp.sum(grad_middle * normed, axis=0, keepdims=True)
    branch_low = low_of(rms_back_of(grad_middle * gains_ref[1:2, :], normed, inverse))
    turned = branch_low.T
    for at in range(0, q_width, tile):
        dwa[:, split_qkv + at : split_qkv + at + tile] = low_of(
            jnp.dot(turned, mixed[:, at : at + tile], preferred_element_type=jnp.float32)
        )
    yield times[1]
    grad_mixed = low_of(
        jnp.dot(branch_low, flat(weights[:, :, split_qkv:]), preferred_element_type=jnp.float32)
    )
    keys = flat(kv_all[:, :, :HEAD])
    values = flat(kv_all[:, :, HEAD:])
    for head in range(HEADS):
        at = head * HEAD
        grad_out = grad_mixed[:, at : at + HEAD]
        share = probs[head]
        grad_share = nt_dot(grad_out, values)
        delta = jnp.sum(share * grad_share, axis=-1, keepdims=True)
        score_grad = low_of(share * (grad_share - delta))
        grad_q[:, at : at + HEAD] = jnp.dot(score_grad, keys, preferred_element_type=jnp.float32)
        key_part = jnp.dot(
            score_grad.T, q_low[:, at : at + HEAD], preferred_element_type=jnp.float32
        )
        value_part = jnp.dot(low_of(share).T, grad_out, preferred_element_type=jnp.float32)
        if head == 0:
            grad_kv[:, :HEAD] = key_part
            grad_kv[:, HEAD:] = value_part
        else:
            grad_kv[:, :HEAD] += key_part
            grad_kv[:, HEAD:] += value_part
        if head == 1:
            yield times[2]
    kv_out[...] = low_of(grad_kv[: REACH * rows, :]).reshape(kv_out.shape)
    sent = [
        copies.start(kv_out.at[REACH - step], kv_in.at[REACH - step], block_peer(-step))
        for step in range(1, REACH + 1)
    ]
    yield times[3]
    for copy in sent:
        copy.wait_recv()
    grad_own = grad_kv[REACH * rows :, :]
    for step in range(REACH):
        grad_own += wide(kv_in[step])
    for head in range(HEADS + 1):
        at = head * HEAD
        which = 0 if head < HEADS else 1
        raw_part = raw[:, at : at + HEAD]
        inverse = inverse_rms(raw_part)
        normed = raw_part * inverse
        if head < HEADS:
            grad_turned = wide(low_of(grad_q[:, at : at + HEAD])) * HEAD ** (-0.5)
        else:
            grad_turned = wide(low_of(grad_own[:, :HEAD]))
        grad = turn_back(grad_turned, cos_ref, sin_ref)
        row = jnp.sum(grad * normed, axis=0, keepdims=True)
        small[4:5, which * HEAD : (which + 1) * HEAD] += row
        proj[:, at : at + HEAD] = low_of(
            rms_back_of(grad * qk_ref[which : which + 1, :], normed, inverse)
        )
    proj[:, q_width + HEAD :] = low_of(grad_own[:, HEAD:])
    inputs = wide(tokens_ref[...])
    inverse = inverse_rms(inputs)
    normed = inputs * inverse
    turned = low_of(normed * gains_ref[0:1, :]).T
    for at in range(0, split_qkv, tile):
        dwa[:, at : at + tile] = low_of(
            jnp.dot(turned, proj[:, at : at + tile], preferred_element_type=jnp.float32)
        )
    grad_in = nt_dot(proj[...], flat(weights[:, :, :split_qkv]))
    small[0:1, :] = jnp.sum(grad_in * normed, axis=0, keepdims=True)
    tokens_grad_ref[...] = grad_middle_ref[...] + rms_back_of(
        grad_in * gains_ref[0:1, :], normed, inverse
    )


def reduce_group_flow(copies, times, group, source, ztrans, zin, zout, yin, yout, gathered, out_ref):
    z_right, z_left, _ = ring_peers("z")
    flip, beside, _ = column_peers()
    chip_z, half = lax.axis_index("z"), lax.axis_index("h")
    part = source.shape[0] // 8

    def rows(z_step, place):
        block = lax.rem(chip_z + z_step, CHIPS) * 2 + place
        return pl.ds(pl.multiple_of(block * part, part), part)

    yield times[0]
    far_r = copies.start(source.at[rows(2, 0)], ztrans.at[0], z_right)
    far_l = copies.start(source.at[rows(2, 1)], ztrans.at[1], z_left)
    plain_r = copies.start(source.at[rows(1, 1)], zin.at[0, 1], z_right)
    plain_l = copies.start(source.at[rows(3, 0)], zin.at[1, 0], z_left)
    yield times[1]
    far_r.wait_recv()
    zout[0] = low_of(wide(source[rows(1, 0), :]) + wide(ztrans[0]))
    sum_r = copies.start(zout.at[0], zin.at[0, 0], z_right)
    far_l.wait_recv()
    zout[1] = low_of(wide(source[rows(3, 1), :]) + wide(ztrans[1]))
    sum_l = copies.start(zout.at[1], zin.at[1, 1], z_left)
    yield times[2]
    plain_r.wait_recv()
    plain_l.wait_recv()
    sum_r.wait_recv()
    sum_l.wait_recv()
    yout[0] = low_of(
        wide(source[rows(0, 1 - half), :]) + wide(zin[0, 1 - half]) + wide(zin[1, 1 - half])
    )
    over = copies.start(yout.at[0], yin.at[0], flip)
    yield times[3]
    over.wait_recv()
    own = wide(source[rows(0, half), :]) + wide(zin[0, half]) + wide(zin[1, half]) + wide(yin[0])
    yout[1] = low_of(own)
    next_to = copies.start(yout.at[1], yin.at[1], beside)
    yield from spread_group(copies, times[4:], group, next_to, yin, yout, gathered, out_ref)


def flip_group_flow(copies, times, group, source, flipped, ztrans, zin, zout, yin, yout, gathered, out_ref):
    z_right, z_left, _ = ring_peers("z")
    flip, beside, _ = column_peers()
    chip_z, half = lax.axis_index("z"), lax.axis_index("h")
    part = source.shape[0] // 8
    top, rest = pl.ds(0, SPLIT), pl.ds(SPLIT, part - SPLIT)
    short = pl.ds(0, part - SPLIT)

    def block(z_step):
        return lax.rem(chip_z + z_step, CHIPS)

    def rows(z_step, place):
        return pl.ds(pl.multiple_of((block(z_step) * 2 + place) * part, part), part)

    order = (2, 1, 3, 0)
    yield times[0]
    over = [
        copies.start(source.at[rows(step, 1 - half)], flipped.at[block(step)], flip) for step in order
    ]
    yield times[1]
    for step, copy in zip(order, over):
        copy.wait_recv()
        flipped[block(step)] = low_of(
            wide(source[rows(step, half), :]) + wide(flipped[block(step)])
        )
    far_r = copies.start(flipped.at[block(2), top], ztrans.at[0, top], z_right)
    far_l = copies.start(flipped.at[block(2), rest], ztrans.at[1, short], z_left)
    plain_r = copies.start(flipped.at[block(1), rest], zin.at[0, 0, rest], z_right)
    plain_l = copies.start(flipped.at[block(3), top], zin.at[1, 0, top], z_left)
    yield times[2]
    far_r.wait_recv()
    zout[0, top, :] = low_of(wide(flipped[block(1), top, :]) + wide(ztrans[0, top, :]))
    sum_r = copies.start(zout.at[0, top], zin.at[0, 0, top], z_right)
    far_l.wait_recv()
    zout[1, short, :] = low_of(wide(flipped[block(3), rest, :]) + wide(ztrans[1, short, :]))
    sum_l = copies.start(zout.at[1, short], zin.at[1, 0, rest], z_left)
    yield times[3]
    for copy in (plain_r, plain_l, sum_r, sum_l):
        copy.wait_recv()
    yout[1] = low_of(wide(flipped[block(0)]) + wide(zin[0, 0]) + wide(zin[1, 0]))
    next_to = copies.start(yout.at[1], yin.at[1], beside)
    yield from spread_group(copies, times[4:], group, next_to, yin, yout, gathered, out_ref)


def spread_group(copies, times, group, next_to, yin, yout, gathered, out_ref):
    x_right, x_left, _ = ring_peers("x")
    chip_x, core = lax.axis_index("x"), lax.axis_index("c")
    sibling = {"c": 1 - core}
    part = yout.shape[1]
    yield times[0]
    next_to.wait_recv()

    def slot(x_step, of_core):
        return lax.rem(chip_x + x_step, CHIPS) * 2 + of_core

    mine = slot(0, core)
    split = 80
    gathered[mine] = low_of(wide(yout[1]) + wide(yin[1]))
    from_left = copies.start(gathered.at[mine], gathered.at[mine], x_right)
    from_right = copies.start(gathered.at[mine], gathered.at[mine], x_left)
    shared = [copies.start(gathered.at[mine], gathered.at[mine], sibling)]
    yield times[1]
    from_left.wait_recv()
    seen = slot(3, core)
    far_first = copies.start(
        gathered.at[seen, pl.ds(0, split)], gathered.at[seen, pl.ds(0, split)], x_right
    )
    shared.append(copies.start(gathered.at[seen], gathered.at[seen], sibling))
    from_right.wait_recv()
    seen = slot(1, core)
    rest = pl.ds(split, part - split)
    far_second = copies.start(gathered.at[seen, rest], gathered.at[seen, rest], x_left)
    shared.append(copies.start(gathered.at[seen], gathered.at[seen], sibling))
    yield times[2]
    far_first.wait_recv()
    far_second.wait_recv()
    seen = slot(2, core)
    shared.append(copies.start(gathered.at[seen], gathered.at[seen], sibling))
    yield times[3]
    for copy in shared:
        copy.wait_recv()
    width = yout.shape[2]
    own_rows = part // 2
    for place in range(8):
        values = wide(gathered[place])
        picked = low_of(jnp.where(core == 0, values[:own_rows], values[own_rows:]))
        for tile in range(0, width, LANES):
            if group == 2:
                which, at = 2, place * width + tile
            else:
                number = (group * width + tile) // LANES
                which, at = number % 2, place * width + number // 2 * LANES
            if at < FF:
                first = which * FF + at
                out_ref[:, first : first + LANES] = picked[:, tile : tile + LANES]


def reduce_attn_flow(copies, times, source, base, cin, xtrans, xin, xout, zin, zown, yin, yown, gathered, other, out_ref):
    x_peers, z_peers, y_peers = ring_peers("x"), ring_peers("z"), column_peers()
    chip_x, chip_z, core, half = (
        lax.axis_index("x"),
        lax.axis_index("z"),
        lax.axis_index("c"),
        lax.axis_index("h"),
    )
    sibling = {"c": 1 - core}
    part, width = source.shape[0] // 8, cin.shape[2]
    cols = width // CHIPS
    span = pl.ds(base, width)

    def rows(block, place):
        return pl.ds(pl.multiple_of((block * 2 + place) * part, part), part)

    def columns(x_step):
        return pl.ds(pl.multiple_of(lax.rem(chip_x + x_step, CHIPS) * cols, cols), cols)

    yield times[0]
    given = [
        copies.start(source.at[rows(b, 1 - core), span], cin.at[b], sibling) for b in range(4)
    ]
    yield times[1]
    for b in range(4):
        given[b].wait_recv()
        cin[b] = low_of(wide(source[rows(b, core), span]) + wide(cin[b]))
    front, back = pl.ds(0, 2), pl.ds(2, 2)
    far_r = copies.start(cin.at[front, :, columns(2)], xtrans.at[0], x_peers[0])
    far_l = copies.start(cin.at[back, :, columns(2)], xtrans.at[1], x_peers[1])
    plain_r = copies.start(cin.at[back, :, columns(1)], xin.at[0, back], x_peers[0])
    plain_l = copies.start(cin.at[front, :, columns(3)], xin.at[1, front], x_peers[1])
    yield times[2]
    far_r.wait_recv()
    xout[0] = low_of(wide(cin[front, :, columns(1)]) + wide(xtrans[0]))
    sum_r = copies.start(xout.at[0], xin.at[0, front], x_peers[0])
    far_l.wait_recv()
    xout[1] = low_of(wide(cin[back, :, columns(3)]) + wide(xtrans[1]))
    sum_l = copies.start(xout.at[1], xin.at[1, back], x_peers[1])
    yield times[3]
    for copy in (plain_r, plain_l, sum_r, sum_l):
        copy.wait_recv()
    zown[...] = low_of(wide(cin[:, :, columns(0)]) + wide(xin[0]) + wide(xin[1]))
    spread = [
        copies.start(zown.at[lax.rem(chip_z + step, CHIPS)], zin.at[place], z_peers[place])
        for place, step in ((0, 1), (1, 3), (2, 2))
    ]
    yield times[4]
    for copy in spread:
        copy.wait_recv()
    yown[...] = low_of(wide(zown[chip_z]) + wide(zin[0]) + wide(zin[1]) + wide(zin[2]))
    spread = [copies.start(yown, yin.at[place], y_peers[place]) for place in range(3)]
    yield times[5]
    for copy in spread:
        copy.wait_recv()
    gathered[chip_x] = low_of(wide(yown[...]) + wide(yin[0]) + wide(yin[1]) + wide(yin[2]))
    spread = [
        copies.start(gathered.at[chip_x], gathered.at[chip_x], x_peers[place]) for place in range(3)
    ]
    yield times[6]
    for copy in spread:
        copy.wait_recv()
    crossing = copies.start(gathered, other, sibling)
    yield times[7]
    crossing.wait_recv()
    own_rows = part // 2
    for place in range(CHIPS):
        values = jnp.where(half == core, wide(gathered[place]), wide(other[place]))
        out_ref[:, base + place * cols : base + (place + 1) * cols] = low_of(
            jnp.where(core == 0, values[:own_rows], values[own_rows:])
        )


def reduce_small_flow(copies, begin, source, cin, held, xin, yin, zin, out_ref):
    core = lax.axis_index("c")
    yield begin
    crossing = copies.start(source, cin, {"c": 1 - core})
    yield begin + 5
    crossing.wait_recv()
    held[0] = source[...] + cin[...]
    for number, (peers, inbox) in enumerate(
        ((ring_peers("x"), xin), (ring_peers("z"), zin), (column_peers(), yin))
    ):
        spread = [copies.start(held.at[number], inbox.at[place], peers[place]) for place in range(3)]
        yield begin + 9 + 4 * number
        for copy in spread:
            copy.wait_recv()
        total = held[number] + inbox[0] + inbox[1] + inbox[2]
        if number < 2:
            held[number + 1] = total
        else:
            out_ref[...] = total


def reduce_kernel(
    gu_ref, down_ref, grad_hidden_ref, po_ref, cot_ref, tokens_ref, weights, cos_ref, sin_ref,
    gains_ref, qk_ref, raw, q_low, kv_all, probs, mixed, branch_ref, middle_ref,
    mlp_out, attn_out, small_out, tokens_grad_ref,
    ztrans, zin, zout, yin, yout, gathered, flipped,
    o_cin, o_xtrans, o_xin, o_xout, o_zin, o_zown, o_yin, o_yown, o_gathered, o_other,
    a_cin, a_xtrans, a_xin, a_xout, a_zin, a_zown, a_yin, a_yown, a_gathered, a_other,
    s_cin, s_held, s_xin, s_yin, s_zin,
    dwa, s_source, grad_kv, kv_out, kv_in, grad_q, grad_middle_ref, proj,
    mlp_sends, mlp_recvs, attn_sends, attn_recvs, small_sends, small_recvs, kv_sends, kv_recvs,
):
    core = lax.axis_index("c")
    a_buffers = (
        (o_cin, o_xtrans, o_xin, o_xout, o_zin, o_zown, o_yin, o_yown, o_gathered, o_other),
        (a_cin, a_xtrans, a_xin, a_xout, a_zin, a_zown, a_yin, a_yown, a_gathered, a_other),
    )
    meet(
        ({"c": 1 - core},) + ring_peers("x") + ring_peers("z") + column_peers()
        + tuple(block_peer(step) for step in range(-REACH, REACH) if step)
    )
    width = down_ref.shape[1]
    sources = (
        gu_ref.at[:, pl.ds(0, width)],
        gu_ref.at[:, pl.ds(width, width)],
        down_ref,
    )
    groups = [Copies(mlp_sends.at[n], mlp_recvs.at[n]) for n in range(3)]
    attn = [Copies(attn_sends.at[n], attn_recvs.at[n]) for n in range(2)]
    small = Copies(small_sends, small_recvs)
    blocks = Copies(kv_sends, kv_recvs)
    flows = [
        attention_back_flow(
            blocks, (1, 6, 8.5, 22), grad_hidden_ref, po_ref, cot_ref, tokens_ref, weights, cos_ref, sin_ref,
            (gains_ref, qk_ref, raw, q_low, kv_all, probs, mixed, branch_ref, middle_ref),
            dwa, s_source, grad_kv, kv_out, kv_in, grad_q, grad_middle_ref, proj, tokens_grad_ref,
        ),
        reduce_small_flow(small, 29, s_source, s_cin, s_held, s_xin, s_yin, s_zin, small_out),
    ]
    split_qkv = (HEADS + 2) * HEAD
    for n, (base, times) in enumerate(
        (
            (split_qkv, (5, 8, 20, 32, 39, 46, 53, 56)),
            (0, (28.5, 34, 46, 56, 63, 70, 77, 80)),
        )
    ):
        flows.append(reduce_attn_flow(attn[n], times, dwa, base, *a_buffers[n], attn_out))
    schedule = (
        (0, 14.5, 33, 41, 49, 57, 62, 65),
        (8.4, 30, 43, 51, 59, 67, 72, 75),
        (0.2, 31, 45, 52, 60, 68, 73, 77),
    )
    for n, group in enumerate((2, 0, 1)):
        shared = (ztrans.at[n], zin.at[n], zout.at[n], yin.at[n], yout.at[n], gathered.at[n], mlp_out)
        if n < 2:
            flow = reduce_group_flow(groups[n], schedule[n], group, sources[group], *shared)
        else:
            flow = flip_group_flow(groups[n], schedule[n], group, sources[group], flipped, *shared)
        flows.append(flow)
    run_flows(flows)
    for copies in groups + attn + [small, blocks]:
        copies.finish()


def reduce_call(w_gu_grad, w_down_grad, operands):
    depth, width = w_down_grad.shape
    weights, tokens = operands[4], operands[3]
    attn_width = weights.shape[2]
    rows, model_width = tokens.shape
    part = depth // 8
    bf16, f32 = jnp.bfloat16, jnp.float32

    def buffer(*shape):
        return pltpu.VMEM(shape, bf16)

    def wide_buffer(*shape):
        return pltpu.VMEM(shape, f32)

    def attn_buffers(columns):
        cols = columns // CHIPS
        return [
            buffer(4, part, columns),
            buffer(2, 2, part, cols),
            buffer(2, 4, part, cols),
            buffer(2, 2, part, cols),
            buffer(3, part, cols),
            buffer(4, part, cols),
            buffer(3, part, cols),
            buffer(part, cols),
            buffer(CHIPS, part, cols),
            buffer(CHIPS, part, cols),
        ]

    def sems(*shape):
        return [pltpu.SemaphoreType.DMA(shape)] * 2

    return pl.pallas_call(
        reduce_kernel,
        out_shape=(
            jax.ShapeDtypeStruct((part // 2, 3 * FF), bf16),
            jax.ShapeDtypeStruct((part // 2, attn_width), bf16),
            jax.ShapeDtypeStruct((8, model_width), f32),
            jax.ShapeDtypeStruct((rows, model_width), f32),
        ),
        in_specs=[vmem_spec()] * (2 + len(operands)),
        out_specs=tuple([vmem_spec()] * 4),
        scratch_shapes=[
            buffer(3, 2, part, width),
            buffer(3, 2, 2, part, width),
            buffer(3, 2, part, width),
            buffer(3, 2, part, width),
            buffer(3, 2, part, width),
            buffer(3, 8, part, width),
            buffer(CHIPS, part, width),
        ]
        + attn_buffers(HEADS * HEAD)
        + attn_buffers((HEADS + 2) * HEAD)
        + [
            wide_buffer(8, model_width),
            wide_buffer(3, 8, model_width),
            wide_buffer(3, 8, model_width),
            wide_buffer(3, 8, model_width),
            wide_buffer(3, 8, model_width),
            buffer(depth, attn_width),
            wide_buffer(8, model_width),
            wide_buffer((REACH + 1) * rows, 2 * HEAD),
            buffer(REACH, rows, 2 * HEAD),
            buffer(REACH, rows, 2 * HEAD),
            wide_buffer(rows, HEADS * HEAD),
            wide_buffer(rows, model_width),
            buffer(rows, (HEADS + 2) * HEAD),
        ]
        + sems(3, 20) + sems(2, 20) + sems(10) + sems(REACH),
        compiler_params=pltpu.CompilerParams(
            collective_id=1, has_side_effects=True, vmem_limit_bytes=63 * 1024 * 1024
        ),
        cost_estimate=pl.CostEstimate(flops=10_000_000, bytes_accessed=20_000_000, transcendentals=0),
        name="attend_back_and_reduce",
    )(w_gu_grad, w_down_grad, *operands)


SPLIT = 80


def plane_gather_flow(copies, times, slots, windows, shared, ready):
    z_right, z_left, _ = ring_peers("z")
    flip, beside, _ = column_peers()
    chip_z, half = lax.axis_index("z"), lax.axis_index("h")
    count = slots.shape[1]
    along = windows + ([shared[0]] if shared else [])
    handed = []

    def send(step, of_half, window, peer, first=0, size=count):
        slot = lax.rem(chip_z + step, CHIPS) * 2 + of_half
        place = slots.at[slot, pl.ds(first, size), window]
        return copies.start(place, place, peer)

    def both(step, of_half):
        return [[send(step, of_half, window, peer) for window in along] for peer in (z_right, z_left)]

    def wait(group):
        for copy in group:
            copy.wait_recv()

    def hand(step, of_half):
        if shared:
            handed.append(send(step, of_half, shared[0], beside))

    def onward(arrived_left, arrived_right, of_half):
        wait(arrived_left)
        first = [send(3, of_half, window, z_right, 0, SPLIT) for window in along]
        hand(3, of_half)
        wait(arrived_right)
        second = [send(1, of_half, window, z_left, SPLIT, count - SPLIT) for window in along]
        hand(1, of_half)
        return first + second

    yield times[0]
    own_right, own_left = both(0, half)
    over = [send(0, half, window, flip) for window in along + ([shared[1]] if shared else [])]
    yield times[1]
    wait(over[: len(along)])
    flip_right, flip_left = both(0, 1 - half)
    yield times[2]
    far = onward(own_right, own_left, half)
    yield times[3]
    far += onward(flip_right, flip_left, 1 - half)
    yield times[4]
    wait(far)
    hand(2, half)
    hand(2, 1 - half)
    yield times[5]
    wait(handed)
    wait(over[len(along) :])
    ready()


def gather_kernel(
    attn_ref, mlp_ref, small_ref, tokens_ref, cos_ref, sin_ref,
    attn_out, mlp_out, gains_out, qk_out, raw, q_low, kv_all, probs, mixed, branch, middle, hidden,
    small_out, shard, a_cin, m_cin, load_sem, sends, recvs,
):
    core, chip_x = lax.axis_index("c"), lax.axis_index("x")
    chip_z, half = lax.axis_index("z"), lax.axis_index("h")
    sibling = {"c": 1 - core}
    x_right, x_left, _ = ring_peers("x")
    z_peers = ring_peers("z")
    flip, _, _ = column_peers()
    load = pltpu.make_async_copy(mlp_ref, shard.at[:, pl.ds(0, mlp_ref.shape[1])], load_sem)
    load.start()
    own_rows = attn_ref.shape[0]
    width = mlp_out.shape[2] // 3
    qkv_half = (HEADS + 2) * HEAD // 2
    out_half = HEADS * HEAD // 2
    qkv = (HEADS + 2) * HEAD
    mine = chip_z * 2 + half
    groups = [Copies(sends.at[n], recvs.at[n]) for n in range(6)]
    first_copies, out_copies, mlp_copies, small_copies, block_copies, late_copies = groups
    meet(
        (sibling, x_right, x_left) + z_peers + (flip,)
        + tuple(block_peer(step) for step in range(-REACH, REACH) if step)
    )

    def lanes(at, size):
        return pl.ds(pl.multiple_of(at, LANES), size)

    def merged(own, other):
        return jnp.where(
            core == 0,
            jnp.concatenate([own, other], axis=0),
            jnp.concatenate([other, own], axis=0),
        )

    small_out[mine * 2 + core] = small_ref[...]
    small_pair = small_copies.start(
        small_out.at[mine * 2 + core], small_out.at[mine * 2 + core], sibling
    )
    given = [
        first_copies.start(
            attn_ref.at[:, lanes((1 - core) * qkv_half, qkv_half)], a_cin.at[:, pl.ds(0, qkv_half)], sibling
        ),
        first_copies.start(
            attn_ref.at[:, lanes(qkv + (1 - core) * out_half, out_half)],
            a_cin.at[:, pl.ds(qkv_half, out_half)],
            sibling,
        ),
    ]
    for copy in given:
        copy.wait_recv()
    for base, at, start, size in (
        (core * qkv_half, 0, 0, 2 * LANES),
        (core * qkv_half, (2 + chip_x) * LANES, 0, LANES),
        (qkv + core * out_half, 0, qkv_half, out_half),
    ):
        own = wide(attn_ref[:, lanes(base + at, size)])
        other = wide(a_cin[:, lanes(start + at, size)])
        attn_out[mine, :, lanes(base + at, size)] = low_of(merged(own, other))
    direct = lanes(core * qkv_half, 2 * LANES)

    def quarter(x_step):
        place = lax.rem(chip_x + x_step, CHIPS)
        return lanes(core * qkv_half + 2 * LANES + place * LANES, LANES)

    def nothing():
        return None

    turn_of = lax.rem(half + lax.axis_index("l"), 2)

    def shared_pair(base, size):
        return (lanes(base + turn_of * size, size), lanes(base + (1 - turn_of) * size, size))

    out_windows = shared_pair(qkv + core * out_half, out_half // 2)
    unshared = 5 * LANES
    mlp_windows = shared_pair(0, unshared)

    def x_flow():
        yield 14.2
        everywhere = pl.ds(0, 8)
        own = attn_out.at[everywhere, :, quarter(0)]
        to_right = first_copies.start(own, own, x_right)
        to_left = first_copies.start(own, own, x_left)
        kept = attn_out.at[everywhere, :, direct]
        shared = [first_copies.start(kept, kept, sibling)]
        yield 23
        to_right.wait_recv()
        near = attn_out.at[pl.ds(0, 4), :, quarter(3)]
        far = [first_copies.start(near, near, x_right)]
        to_left.wait_recv()
        near = attn_out.at[pl.ds(4, 4), :, quarter(1)]
        far.append(first_copies.start(near, near, x_left))
        yield 28
        for copy in far:
            copy.wait_recv()
        rest = attn_out.at[everywhere, :, lanes(core * qkv_half + 2 * LANES, 4 * LANES)]
        shared.append(first_copies.start(rest, rest, sibling))
        yield 31
        for copy in shared:
            copy.wait_recv()

    shares = []

    def share_out():
        place = attn_out.at[pl.ds(0, 8), :, lanes(qkv + core * out_half, out_half)]
        shares.append(out_copies.start(place, place, sibling))

    def out_flow():
        yield 47.5
        for copy in shares:
            copy.wait_recv()

    def mlp_exchange():
        yield 3
        load.wait()
        shard[:, pl.ds(mlp_ref.shape[1], shard.shape[1] - mlp_ref.shape[1])] = jnp.zeros(
            (own_rows, shard.shape[1] - mlp_ref.shape[1]), shard.dtype
        )
        part = chip_x * 2
        given = [
            mlp_copies.start(
                shard.at[:, lanes(n * FF + (part + 1 - core) * width, width)], m_cin.at[n], sibling
            )
            for n in range(3)
        ]
        yield 4
        for n in range(3):
            given[n].wait_recv()
            own = wide(shard[:, lanes(n * FF + (part + core) * width, width)])
            block = low_of(merged(own, wide(m_cin[n])))
            if n == 2:
                mlp_out[mine, :, 2 * width :] = block
            else:
                for at in range(0, width, LANES):
                    here = 2 * at + n * LANES
                    mlp_out[mine, :, here : here + LANES] = block[:, at : at + LANES]

    def gains_of():
        own_width, own_qk = gains_out.shape[1] // 16, qk_out.shape[1] // 16
        gains_out[...] = jnp.concatenate(
            [small_out[place][:, :own_width] for place in range(16)], axis=1
        )
        qk_out[...] = jnp.concatenate(
            [small_out[place][4:6, :own_qk] for place in range(16)], axis=1
        )

    def small_flow():
        yield 2
        small_pair.wait_recv()
        place = small_out.at[pl.ds(mine * 2, 2)]
        over = small_copies.start(place, place, flip)
        yield 4.5
        over.wait_recv()
        place = small_out.at[pl.ds(chip_z * 4, 4)]
        spread = [small_copies.start(place, place, peer) for peer in z_peers]
        yield 8
        for copy in spread:
            copy.wait_recv()

    run_flows(
        [
            plane_gather_flow(
                first_copies, (0, 7, 8, 11, 14, 14.1), attn_out, [direct, quarter(0)], None, nothing
            ),
            x_flow(),
            small_flow(),
            plane_gather_flow(
                out_copies, (8.1, 14.5, 15, 18, 21, 29), attn_out, [], out_windows, share_out,
            ),
            mlp_exchange(),
            plane_gather_flow(
                mlp_copies, (8.2, 19, 20, 24, 30, 59), mlp_out, [], mlp_windows, nothing
            ),
            plane_gather_flow(
                late_copies, (14.3, 26, 29, 42.5, 47, 60), mlp_out,
                [pl.ds(2 * unshared, 3 * width - 2 * unshared)], None,
                nothing,
            ),
            attention_flow(
                block_copies, (31.5, 42, 48), attn_out, gains_of, tokens_ref, cos_ref, sin_ref,
                (gains_out, qk_out, raw, q_low, kv_all, probs, mixed, branch, middle, hidden),
            ),
            out_flow(),
        ]
    )
    for copies in groups:
        copies.finish()


def gather_call(w_attn, w_mlp, small, tokens, cos_table, sin_table, slice_width):
    own_rows, attn_width = w_attn.shape
    rows, model_width = tokens.shape
    bf16, f32 = jnp.bfloat16, jnp.float32
    return pl.pallas_call(
        gather_kernel,
        out_shape=(
            jax.ShapeDtypeStruct((8, 2 * own_rows, attn_width), bf16),
            jax.ShapeDtypeStruct((8, 2 * own_rows, 3 * slice_width), bf16),
            jax.ShapeDtypeStruct((8, model_width), f32),
            jax.ShapeDtypeStruct((2, HEAD), f32),
            jax.ShapeDtypeStruct((rows, (HEADS + 1) * HEAD), f32),
            jax.ShapeDtypeStruct((rows, HEADS * HEAD), bf16),
            jax.ShapeDtypeStruct((REACH + 1, rows, 2 * HEAD), bf16),
            jax.ShapeDtypeStruct((HEADS, rows, (REACH + 1) * rows), f32),
            jax.ShapeDtypeStruct((rows, HEADS * HEAD), bf16),
            jax.ShapeDtypeStruct((rows, model_width), f32),
            jax.ShapeDtypeStruct((rows, model_width), f32),
            jax.ShapeDtypeStruct((rows, model_width), bf16),
        ),
        in_specs=[vmem_spec(), pl.BlockSpec(memory_space=pl.ANY)] + [vmem_spec()] * 4,
        out_specs=tuple([vmem_spec()] * 12),
        scratch_shapes=[
            pltpu.VMEM((16,) + small.shape, f32),
            pltpu.VMEM((own_rows, 2 * FF + 8 * slice_width), bf16),
            pltpu.VMEM((own_rows, attn_width // 2), bf16),
            pltpu.VMEM((3, own_rows, slice_width), bf16),
            pltpu.SemaphoreType.DMA,
            pltpu.SemaphoreType.DMA((6, 28)),
            pltpu.SemaphoreType.DMA((6, 28)),
        ],
        compiler_params=pltpu.CompilerParams(
            collective_id=2, has_side_effects=True, vmem_limit_bytes=60 * 1024 * 1024
        ),
        cost_estimate=pl.CostEstimate(flops=10_000_000, bytes_accessed=20_000_000, transcendentals=0),
        name="gather_and_attend",
    )(w_attn, w_mlp, small, tokens, cos_table, sin_table)


def shards(tokens, w_attn, w_mlp, norm_gains, qk_gains, cotangent):
    seq_count, block_len, model_width = tokens.shape
    row_count = seq_count * block_len
    seq_index = lax.axis_index("x") * 2 + lax.axis_index("l")
    slice_width = -(-FF // (8 * LANES)) * LANES
    inputs = tokens.reshape(row_count, model_width)
    grad_out = cotangent.reshape(row_count, model_width)
    own_width, own_qk = norm_gains.shape[1], qk_gains.shape[1]
    small = jnp.concatenate(
        [
            jnp.pad(norm_gains.astype(jnp.float32), ((0, 0), (0, LANES - own_width))),
            jnp.pad(qk_gains.astype(jnp.float32), ((0, 2), (0, LANES - own_qk))),
        ],
        axis=0,
    )
    positions = (seq_index * block_len + jnp.arange(block_len, dtype=jnp.int32)).astype(jnp.float32)
    half_size = HEAD // 2
    frequency = ROPE_BASE ** (-(jnp.arange(half_size, dtype=jnp.float32) * 2.0) / HEAD)
    angles = positions[:, None] * frequency[None, :]
    tables = (jnp.cos(angles), jnp.sin(angles))
    attn_full, mlp_part, gains, qk, raw, q_low, kv_all, probs, mixed, branch, middle, hidden = (
        gather_call(w_attn, w_mlp, small, inputs, *tables, slice_width)
    )
    result, grad_hidden, gain_row, upper_part, lower_part = mlp_call(
        hidden,
        middle,
        grad_out,
        mlp_part.reshape(model_width, 3 * slice_width),
        gains[3:4],
    )
    mlp_total, attn_total, small, grad_inputs = reduce_call(
        upper_part,
        lower_part,
        (grad_hidden, gain_row, grad_out, inputs, attn_full, *tables, gains, qk, raw, q_low, kv_all)
        + (probs, mixed, branch, middle),
    )
    fsdp_index = lax.axis_index(("z", "h", "c"))
    gain_total = lax.dynamic_slice_in_dim(small[:4], fsdp_index * own_width, own_width, axis=1)
    qk_total = lax.dynamic_slice_in_dim(
        small[4, : 2 * HEAD].reshape(2, HEAD), fsdp_index * own_qk, own_qk, axis=1
    )
    return (
        result.reshape(tokens.shape),
        grad_inputs.reshape(tokens.shape),
        attn_total.astype(jnp.float32),
        mlp_total.astype(jnp.float32),
        gain_total,
        qk_total,
    )


def solution(mesh):
    fine = Mesh(mesh.devices.reshape(4, 2, 4, 2, 2), ("x", "l", "z", "h", "c"))
    fsdp = ("z", "h", "c")
    seq = ("x", "l")
    in_specs = (
        P(fsdp, seq, None),
        P(fsdp, None),
        P(fsdp, None),
        P(None, fsdp),
        P(None, fsdp),
        P(fsdp, seq, None),
    )
    out_specs = (
        P(fsdp, seq, None),
        P(fsdp, seq, None),
        P(fsdp, None),
        P(fsdp, None),
        P(None, fsdp),
        P(None, fsdp),
    )
    return jax.shard_map(shards, mesh=fine, in_specs=in_specs, out_specs=out_specs, check_vma=False)
```

time: 1090 us -> 297 us (0.27)
  waiting for transfers between devices: 752 us -> 0 us
  Pallas kernels: 0 us -> 282 us
  matrix products: 97.8 us -> 0 us
  blocking collectives: 97.6 us -> 0 us
  other arithmetic: 62 us -> 8.12 us
  starting transfers between devices: 35.9 us -> 0 us
  local copies, waits for them, and re-layouts: 23.4 us -> 4.23 us
  between operations: 15.8 us -> 0.71 us
    reduce_scatter x2 -> x0, waiting for transfers between devices: 360 us -> none  [the longest x1 326 us: shards(): lax.psum_scatter(jnp.concatenate([upper_part, lower_part], axis=1).astype...]
    pallas_call x0 -> x3, Pallas kernels: none -> 282 us  [the longest x1 120 us: reduce_call(): pl.pallas_call(reduce_kernel, out_shape=(jax.ShapeDtypeStruct((part // 2,...]
    all_gather x2 -> x0, waiting for transfers between devices: 213 us -> none  [the longest x1 197 us: shards(): mlp_full = lax.all_gather(w_mlp, 'fsdp', axis=0, tiled=True)]
    psum x1 -> x0, waiting for transfers between devices: 133 us -> none  [shards(): lax.psum(attn_part.astype(jnp.bfloat16), 'seq').astype(jnp.float32)]
    dot_general x18 -> x0, matrix products: 97.8 us -> none  [the longest x1 16.3 us: shards(): jnp.einsum('nd,nf->df', hidden_ff, gu_low, preferred_element_type=jnp.flo...]
    all_gather x2 -> x0, blocking collectives: 45.1 us -> none  [the longest x1 24.5 us: shards(): lax.all_gather(norm_gains, 'fsdp', axis=1, tiled=True)]
    ppermute x16 -> x0, starting transfers between devices: 35.6 us -> none  [passed_along(): lax.ppermute(value, axis, [(source, source + steps) for source in range(i...]
    concatenate x4 -> x1, other arithmetic: 36 us -> 1.3 us  [shards(): jnp.concatenate([jnp.pad(norm_gains.astype(jnp.float32), ((0, 0), (0, LAN...]
  transfers between devices with their start and end apart: 22 -> 0, of which waited for: 14 -> 0; matrix products, arithmetic and copies ran while one was open for 8% -> 0% of each run, Pallas kernels for 0% -> 0%
where the time goes in v1:
time: 297 us; the launch traced here: 295 us
  Pallas kernels  282 us (95%)
  other arithmetic  8.12 us (3%)
  local copies, waits for them, and re-layouts  4.23 us (1%)
    pallas_call x1, Pallas kernels, reduce_call(): pl.pallas_call(reduce_kernel, out_shape=(jax.ShapeDtypeStruct((part // 2,...  120 us
    pallas_call x1, Pallas kernels, gather_call(): pl.pallas_call(gather_kernel, out_shape=(jax.ShapeDtypeStruct((8, 2 * own...  83.5 us
    pallas_call x1, Pallas kernels, mlp_call(): pl.pallas_call(mlp_kernel, out_shape=(jax.ShapeDtypeStruct((rows, model_w...  78.9 us

profile of v1, /device:TPU:16, one launch (start us, length us, event | category | flops | bytes accessed | tf_op | source)
XLA Modules:
  0.0 295.3 jit_solution(8977285999525750569)
XLA Ops:
  0.7 1.0 multiply_sine_fusion
  1.6 1.3 fusion.3.small_ref
  2.9 83.5 %gather_and_attend.1 = (bf16[8,144,2560]{2,1,0:T(8,128)(2,1)}, bf16[8,144,2688]{2,1,0:T(8,128)(2,1)}, f32[8,1152]{1,0:T(8,128)}, f32[2,256]{1,0:T(2,128)}, f32[1...) custom-call(bf16[72,2560]{1,0:T(8,128)(2,1)} %attn_ref.1, ...), custom_call_target="tpu_custom_call" | custom-call | flops 10000000 | bytes 20000000 | tf_op jit(solution)/shard_map/gather_and_attend/pallas_call | solution.py:1177
  86.4 1.4 slice.9.gain_ref
  87.8 78.9 %feed_forward.1 = (bf16[128,1152]{1,0:T(8,128)(2,1)}, f32[128,1152]{1,0:T(8,128)}, f32[1,1152]{1,0:T(1,128)}, bf16[1152,1792]{1,0:T(8,128)(2,1)}, bf16[1152,896]{1,0:T(8,128)(2,1)}) custom-call(bf16[128,1152]{1,0:T(8,128)(2,1)} %get-tuple-element.27.hidden_ref, f32[128,1152]{1,0:T(8,128)} %get-tuple-element.28.middle_ref, bf16[128,1152]{1,0:T(8,128)(2,1)} %bitcast.9, ...), custom_call_target="tpu_custom_call" | custom-call | flops 19025362944 | bytes 20000000 | tf_op jit(solution)/shard_map/feed_forward/pallas_call | solution.py:272
  166.7 119.8 %attend_back_and_reduce.1 = (bf16[72,20736]{1,0:T(8,128)(2,1)}, bf16[72,2560]{1,0:T(8,128)(2,1)}, f32[8,1152]{1,0:T(8,128)}, f32[128,1152]{1,0:T(8,128)}) custom-call(bf16[1152,1792]{1,0:T(8,128)(2,1)} %get-tuple-element.32.gu_ref, bf16[1152,896]{1,0:T(8,128)(2,1)} %get-tuple-element.33.down_ref, f32[128,1152]{1,0:T(8,128)} %get-tuple-element.34.grad_hidden_ref, ...), custom_call_target="tpu_custom_call" | custom-call | flops 10000000 | bytes 20000000 | tf_op jit(solution)/shard_map/attend_back_and_reduce/pallas_call | solution.py:882
  286.5 0.0 copy-start.1
  286.6 0.0 copy-start.3
  286.6 0.0 copy-start.2
  286.6 0.0 copy-start
  286.6 4.9 %convert_element_type.21 = f32[72,20736]{1,0:T(8,128)} convert(bf16[72,20736]{1,0:T(8,128)(2,1)} %get-tuple-element.46) | non-fusion elementwise | flops 1492992 | bytes 8957952 | tf_op jit(solution)/shard_map/convert_element_type | solution.py:1257
  291.5 0.0 copy-done.1
  291.5 0.9 convert_element_type.20
  292.4 0.0 copy-done.3
  292.4 0.6 constant_dynamic-slice_fusion.1
  293.1 0.6 constant_dynamic-slice_fusion
  293.8 0.0 copy-done.2
  293.8 0.7 copy.14
  294.5 0.0 copy-done
  294.5 0.8 copy.15
  (5 shorter events, 0.1 us)
Async XLA Ops:
  286.5 5.0 %copy-start.1 = (bf16[72,2560]{1,0:T(8,128)(2,1)S(1)}, bf16[72,2560]{1,0:T(8,128)(2,1)}, u32[]{:S(2)}) copy-start(bf16[72,2560]{1,0:T(8,128)(2,1)} %get-tuple-element.45) | copy-start | bytes 1105924
  286.6 5.9 %copy-start.3 = (f32[8,1152]{1,0:T(8,128)S(1)}, f32[8,1152]{1,0:T(8,128)}, u32[]{:S(2)}) copy-start(f32[8,1152]{1,0:T(8,128)} %get-tuple-element.47) | copy-start | bytes 110596
  286.6 7.2 %copy-start.2 = (bf16[128,1152]{1,0:T(8,128)(2,1)S(1)}, bf16[128,1152]{1,0:T(8,128)(2,1)}, u32[]{:S(2)}) copy-start(bf16[128,1152]{1,0:T(8,128)(2,1)} %get-tuple-element.31) | copy-start | bytes 884740
  286.6 7.9 %copy-start = (f32[128,1152]{1,0:T(8,128)S(1)}, f32[128,1152]{1,0:T(8,128)}, u32[]{:S(2)}) copy-start(f32[128,1152]{1,0:T(8,128)} %get-tuple-element.44) | copy-start | bytes 1769476
